TPU v7x, 32 devices: a whole 2x2x4 slice. The times are simulated.
32 devices in a mesh: groups: 2 (over y), ranks: 8 (over z, x), side: 2 (over core).
Axes of the slice: x: 2, y: 2, z: 4, core: 2. Of those that a mesh axis runs over, the one named last changes fastest.
Arguments:
- queries: bfloat16 [4096, 4096], P(('groups', 'ranks'), 'side'), parts along dimension 0, may hold values from -25 to 25
- keys: bfloat16 [512, 4096], P(('groups', 'ranks'), 'side'), parts along dimension 0, may hold values from -6 to 6
- values: bfloat16 [512, 4096], P(('groups', 'ranks'), 'side'), parts along dimension 0, may hold values from -96 to 96
- residual: bfloat16 [4096, 4096], P(('groups', 'ranks'), 'side'), parts along dimension 0, may hold values from -6 to 6
- merge_map: int32 [4096], P(('groups', 'ranks')), parts along dimension 0, may hold values from 0 to 31, as said below
- expert_ids: int32 [512, 2], P(('groups', 'ranks')), parts along dimension 0, may hold values from 0 to 3, all different within a row; in each aligned block of 32 rows (0 to 31, 32 to 63, ...) at most 32 rows name the same one
- gate_weights: float32 [512, 2], P(('groups', 'ranks')), parts along dimension 0, may hold values from 0.25 to 1
- norm_gain: bfloat16 [4096], P('side'), may hold values from 0.3984375 to 1.59375
- w_gate: bfloat16 [8, 4096, 768], P('ranks', 'side'), may hold values from -0.09375 to 0.09375
- w_up: bfloat16 [8, 4096, 768], P('ranks', 'side'), may hold values from -0.09375 to 0.09375
- w_down: bfloat16 [8, 768, 4096], P('ranks', None, 'side'), may hold values from -0.15625 to 0.15625
Outputs:
- layer_out: bfloat16 [4096, 4096], P(('groups', 'ranks'), 'side'), parts along dimension 0
There are 2 independent parts, one for each index of `groups`. A program takes and returns all parts, laid end to end along the dimension named above; an argument that names none is the same for every part. Nothing has to cross between parts.
Inputs may be any that keep to these rules, and one draw needn't show every extreme that they name: `merge_map`: each merged token m of shard r (r * 32 <= m < (r + 1) * 32) is the group of one or more tokens of shard r. `expert_ids`: the 2 experts of a merged token differ; among the merged tokens of one shard (aligned blocks of 32) no expert is named more than 32 times.
All inputs are finite; a program needn't handle non-finite values.
Results may differ from a plain program's by a relative error of at most 0.0065.
The roundings to bfloat16 on the way count: a program that leaves them out, or rounds other values in their place, can miss the bound.
Values may be sent and summed in bfloat16 or wider, within the bound.
A program may use at most 128 MiB of HBM per device.

v0:
```python
import math

import jax
import jax.numpy as jnp
from jax import lax
from jax.sharding import PartitionSpec as P

D = 4096
HEAD_DIM = 128
TOP = 2


def local(
    queries,
    keys,
    values,
    residual,
    merge_map,
    expert_ids,
    gate_weights,
    norm_gain,
    w_gate,
    w_up,
    w_down,
):
    query_rows, half_width = queries.shape
    head_count = half_width // HEAD_DIM
    merged_rows = keys.shape[0]
    factor = 1.0 / math.sqrt(HEAD_DIM)
    members = (merge_map[:, None] == jnp.arange(merged_rows, dtype=jnp.int32)[None, :]).astype(
        jnp.float32
    )
    member_counts = jnp.sum(members, axis=0)
    key_bias = jnp.log(member_counts).astype(jnp.bfloat16)
    query_heads = queries.reshape(query_rows, head_count, HEAD_DIM)
    all_keys, all_values, all_bias = (
        lax.all_gather(keys, "ranks", axis=0, tiled=True),
        lax.all_gather(values, "ranks", axis=0, tiled=True),
        lax.all_gather(key_bias, "ranks", axis=0, tiled=True),
    )
    count_rows = all_keys.shape[0]
    scores = jnp.einsum(
        "qhd,khd->hqk",
        query_heads,
        all_keys.reshape(count_rows, head_count, HEAD_DIM),
        preferred_element_type=jnp.float32,
    )
    scores = scores * factor + all_bias.astype(jnp.float32)[None, None, :]
    weights = jnp.exp(scores - jnp.max(scores, axis=2, keepdims=True))
    totals = jnp.sum(weights, axis=2)
    weighted_sum = jnp.einsum(
        "hqk,khd->hqd",
        weights.astype(jnp.bfloat16),
        all_values.reshape(-1, head_count, HEAD_DIM),
        preferred_element_type=jnp.float32,
    )
    attended = (
        (weighted_sum / totals[:, :, None]).transpose(1, 0, 2).reshape(query_rows, half_width)
    )
    summed = residual.astype(jnp.float32) + attended
    merged_state = (
        jnp.dot(members.T, summed, precision=lax.Precision.HIGHEST) / member_counts[:, None]
    )
    square_sum = lax.psum(jnp.sum(merged_state * merged_state, axis=1), "side")
    inverse = lax.rsqrt(square_sum / D + 1e-06)
    normed = (merged_state * inverse[:, None] * norm_gain.astype(jnp.float32)[None, :]).astype(
        jnp.bfloat16
    )
    rank_total = lax.axis_size("ranks")
    expert_count = rank_total // 2
    capacity = max(2, 4 * merged_rows // expert_count)
    slot_count = rank_total * capacity
    flat_ids = expert_ids.reshape(-1)
    onehot = (flat_ids[:, None] == jnp.arange(expert_count, dtype=jnp.int32)[None, :]).astype(
        jnp.int32
    )
    position = jnp.sum((jnp.cumsum(onehot, axis=0) - 1) * onehot, axis=1)
    targets = (
        2 * flat_ids[:, None] + jnp.arange(2, dtype=jnp.int32)[None, :]
    ) * capacity + position[:, None]
    slot_hits = (
        jnp.arange(slot_count, dtype=jnp.int32)[:, None, None] == targets[None, :, :]
    ).astype(jnp.float32)
    routed = jnp.sum(slot_hits, axis=2).reshape(slot_count, merged_rows, TOP)
    spread = jnp.sum(routed, axis=2).astype(jnp.bfloat16)
    outgoing = jnp.dot(spread, normed, preferred_element_type=jnp.float32).astype(jnp.bfloat16)
    combine = jnp.einsum("tmk,mk->mt", routed, gate_weights, precision=lax.Precision.HIGHEST)
    incoming = lax.all_to_all(
        outgoing.reshape(rank_total, capacity, half_width),
        "ranks",
        split_axis=0,
        concat_axis=0,
        tiled=True,
    )
    incoming = incoming.reshape(slot_count, half_width)
    gate_part = jnp.dot(incoming, w_gate[0], preferred_element_type=jnp.float32)
    up_part = jnp.dot(incoming, w_up[0], preferred_element_type=jnp.float32)
    gate_proj, up_proj = (
        lax.psum(gate_part.astype(jnp.bfloat16), "side").astype(jnp.float32),
        lax.psum(up_part.astype(jnp.bfloat16), "side").astype(jnp.float32),
    )
    hidden = (jax.nn.silu(gate_proj) * up_proj).astype(jnp.bfloat16)
    partial_out = jnp.dot(hidden, w_down[0], preferred_element_type=jnp.float32)
    returned = lax.all_to_all(
        partial_out.reshape(rank_total, capacity, half_width).astype(jnp.bfloat16),
        "ranks",
        split_axis=0,
        concat_axis=0,
        tiled=True,
    ).astype(jnp.float32)
    expert_out = jnp.dot(
        combine, returned.reshape(slot_count, half_width), precision=lax.Precision.HIGHEST
    )
    layer_out = summed + jnp.dot(members, expert_out, precision=lax.Precision.HIGHEST)
    return layer_out.astype(jnp.bfloat16)


def solution(mesh):
    return jax.shard_map(
        local,
        mesh=mesh,
        in_specs=(
            P(("groups", "ranks"), "side"),
            P(("groups", "ranks"), "side"),
            P(("groups", "ranks"), "side"),
            P(("groups", "ranks"), "side"),
            P(("groups", "ranks")),
            P(("groups", "ranks"), None),
            P(("groups", "ranks"), None),
            P("side"),
            P("ranks", "side", None),
            P("ranks", "side", None),
            P("ranks", None, "side"),
        ),
        out_specs=P(("groups", "ranks"), "side"),
        check_vma=False,
    )
```

profile of v0, /device:TPU:0, one launch (start us, length us, event | category | flops | bytes accessed | tf_op | source)
XLA Modules:
  0.0 208.8 jit_solution(4683278613249258356)
XLA Ops:
  6.5 0.7 all-gather.3.cloned.1.call-update
  7.3 0.7 all-gather.5.cloned.1.call-update
  8.1 0.8 convert_reduce_fusion.1
  8.9 1.2 dynamic-slice
  10.8 0.2 dynamic-update-slice
  11.0 23.1 %all-reduce = bf16[256]{0:T(256)(128)(2,1)S(1)} all-reduce(bf16[256]{0:T(256)(128)(2,1)S(1)} %dynamic-update-slice), channel_id=1, replica_groups=mesh['groups'=2,'ranks'=8,'side'=2] {'ranks'}, use_global_device_ids=true, to_apply=%add | all-reduce | flops 256 | bytes 1024
  34.1 0.8 copy.37
  35.2 0.2 select_reduce_fusion
  35.5 0.7 convert_element_type.63
  36.3 16.1 %all-gather.3.cloned.1.call-done = bf16[256,2048]{1,0:T(8,128)(2,1)} async-done(((bf16[32,2048]{1,0:T(8,128)(2,1)}), bf16[256,2048]{1,0:T(8,128)(2,1)}) %all-gather.3.cloned.1.call-update) | async-done | bytes 1048592 | tf_op jit(solution)/shard_map/all_gather | solution.py:37
  52.4 2.3 %copy.31 = bf16[256,2048]{0,1:T(8,128)(2,1)} copy(bf16[256,2048]{1,0:T(8,128)(2,1)} %all-gather.3.cloned.1.call-done) | data formatting | bytes 2097152 | tf_op jit(solution)/shard_map/all_gather | solution.py:37
  54.7 2.6 %fusion = (f32[16,256]{1,0:T(8,128)S(1)}, f32[16,256,256]{1,2,0:T(8,128)S(1)}) fusion(f32[256]{0:T(256)S(1)} %convert_element_type.58, bf16[256,16,128]{0,2,1:T(8,128)(2,1)} %bitcast.53, bf16[256,2048]{1,0:T(8,128)(2,1)} %param.11), kind=kOutput, calls=%fused_computation.2 | convolution fusion | flops 271577088 | bytes 6308864 | tf_op jit(solution)/shard_map/qhd,khd->hqk/dot_general | solution.py:42
  57.3 1.9 copy-done.1
  59.2 0.9 fusion.1
  60.1 33.4 %all-gather.5.cloned.1.call-done = bf16[256,2048]{1,0:T(8,128)(2,1)} async-done(((bf16[32,2048]{1,0:T(8,128)(2,1)}), bf16[256,2048]{1,0:T(8,128)(2,1)}) %all-gather.5.cloned.1.call-update) | async-done | bytes 1048592 | tf_op jit(solution)/shard_map/all_gather | solution.py:38
  93.5 2.3 %copy.34 = bf16[256,2048]{0,1:T(8,128)(2,1)} copy(bf16[256,2048]{1,0:T(8,128)(2,1)} %all-gather.5.cloned.1.call-done) | data formatting | bytes 2097152 | tf_op jit(solution)/shard_map/all_gather | solution.py:38
  95.7 5.0 %bitcast_divide_fusion = f32[256,16,128]{0,2,1:T(8,128)} fusion(f32[256,16]{0,1:T(8,128)S(1)} %bitcast.59, bf16[256,16,128]{0,2,1:T(8,128)(2,1)} %bitcast.55, f32[16,256,256]{1,2,0:T(8,128)} %copy-done.1, f32[16,256]{1,0:T(8,128)S(1)} %get-tuple-element.7, f32[256]{0:T(256)S(1)} %convert_element_type.58), kind=kOutput, calls=%fused_computation.17 | convolution fusion | flops 273154048 | bytes 7373824 | tf_op jit(solution)/shard_map/hqk,khd->hqd/dot_general | solution.py:51
  100.7 3.0 %copy.36 = f32[256,2048]{1,0:T(8,128)} copy(f32[256,2048]{0,1:T(8,128)} %bitcast.54) | data formatting | bytes 4194304 | tf_op jit(solution)/shard_map/reshape | solution.py:58
  103.7 3.0 %multiply_reduce_fusion = (f32[32]{0:T(128)S(1)}, f32[32,2048]{1,0:T(8,128)S(1)}) fusion(f32[32]{0:T(128)S(1)} %convert_reduce_fusion.1, f32[256,2048]{1,0:T(8,128)} %copy.36, bf16[256,2048]{1,0:T(8,128)(2,1)} %param.14, s32[256]{0:T(256)S(1)} %copy-done.2), kind=kOutput, calls=%fused_computation.35 | convolution fusion | flops 202579936 | bytes 3409152 | tf_op jit(solution)/shard_map/dot_general | solution.py:62
  106.7 2.5 %psum.21 = f32[32]{0:T(128)S(1)} all-reduce(f32[32]{0:T(128)S(1)} %get-tuple-element.9), channel_id=1, replica_groups=mesh['groups'=2,'ranks'=8,'side'=2] {'side'}, use_global_device_ids=true, to_apply=%region_8.9 | all-reduce | flops 32 | bytes 256 | tf_op jit(solution)/shard_map/psum | solution.py:64
  109.1 0.5 convolution_convert_fusion
  109.6 29.3 %all_to_all.10 = bf16[8,32,2048]{2,1,0:T(8,128)(2,1)S(1)} all-to-all(bf16[8,32,2048]{2,1,0:T(8,128)(2,1)S(1)} %bitcast.52), channel_id=1, replica_groups=mesh['groups'=2,'ranks'=8,'side'=2] {'ranks'}, dimensions={0} | all-to-all | bytes 2097152 | tf_op jit(solution)/shard_map/all_to_all | solution.py:88
  139.0 1.7 fusion.18
  140.9 1.7 fusion.21
  142.6 18.5 %all-reduce.4.cloned.1.call-done = (bf16[256,768]{1,0:T(8,128)(2,1)}, bf16[256,768]{1,0:T(8,128)(2,1)}) async-done(((bf16[256,768]{1,0:T(8,128)(2,1)}, bf16[256,768]{1,0:T(8,128)(2,1)}), (bf16[256,768]{1,0:T(8,128)(2,1)}, bf16[256,768]{1,0:T(8,128)(2,1)})) %all-reduce.4.cloned.1.call-update) | async-done | bytes 786448 | tf_op jit(solution)/shard_map/psum | solution.py:100
  161.1 1.4 fusion.33
  162.5 2.0 fusion.10
  164.4 5.8 %all-to-all-start.1 = ((bf16[8,32,2048]{2,1,0:T(8,128)(2,1)}), bf16[8,32,2048]{2,1,0:T(8,128)(2,1)}, u32[]{:S(2)}, u32[]{:S(2)}) async-start(bf16[8,32,2048]{2,1,0:T(8,128)(2,1)} %fusion.10), calls=%async_computation.1 | async-start | bytes 2097152 | tf_op jit(solution)/shard_map/all_to_all | solution.py:104
  170.3 0.4 fusion.44
  170.7 25.9 %all-to-all-done.1 = bf16[8,32,2048]{2,1,0:T(8,128)(2,1)} async-done(((bf16[8,32,2048]{2,1,0:T(8,128)(2,1)}), bf16[8,32,2048]{2,1,0:T(8,128)(2,1)}, u32[]{:S(2)}, u32[]{:S(2)}) %all-to-all-start.1) | async-done | bytes 1048608 | tf_op jit(solution)/shard_map/all_to_all | solution.py:104
  196.5 1.8 fusion.36
  198.4 3.9 %fusion.9 = bf16[256,2048]{1,0:T(8,128)(2,1)} fusion(f32[32,2048]{1,0:T(8,128)S(1)} %fusion.36, f32[256,2048]{1,0:T(8,128)} %copy.36, bf16[256,2048]{1,0:T(8,128)(2,1)} %param.14, s32[256]{0:T(256)S(1)} %copy-done.2), kind=kOutput, calls=%fused_computation.12 | convolution fusion | flops 203431936 | bytes 4457472 | tf_op jit(solution)/shard_map/dot_general | solution.py:114
  (28 shorter events, 0.9 us)
Async XLA Ops:
  6.5 155.9 %copy-start = (bf16[1,768,2048]{2,1,0:T(8,128)(2,1)S(1)}, bf16[1,768,2048]{2,1,0:T(8,128)(2,1)}, u32[]{:S(2)}) copy-start(bf16[1,768,2048]{2,1,0:T(8,128)(2,1)} %param.21) | copy-start | bytes 9437188
  6.5 45.9 %all-gather.3.cloned.1.call-start = ((), (), s32[]{:S(2)}) async-start(), calls=%async_computation.2 | async-start | bytes 1179648 | tf_op jit(solution)/shard_map/all_gather | solution.py:37
  7.3 86.2 %all-gather.5.cloned.1.call-start = ((), (), s32[]{:S(2)}) async-start(), calls=%async_computation.3 | async-start | bytes 1179648 | tf_op jit(solution)/shard_map/all_gather | solution.py:38
  8.0 153.1 %all-reduce.4.cloned.1.call-start = ((), (), s32[]{:S(2)}) async-start(), calls=%async_computation.4 | async-start | bytes 1572864 | tf_op jit(solution)/shard_map/psum | solution.py:100
  57.2 1.9 copy-start.1
  100.7 3.0 %copy-start.2 = (s32[256]{0:T(256)S(1)}, s32[256]{0:T(256)}, u32[]{:S(2)}) copy-start(s32[256]{0:T(256)} %param.15) | copy-start | bytes 3076
  109.1 29.8 %copy-start.4 = (bf16[1,2048,768]{2,1,0:T(8,128)(2,1)S(1)}, bf16[1,2048,768]{2,1,0:T(8,128)(2,1)}, u32[]{:S(2)}) copy-start(bf16[1,2048,768]{2,1,0:T(8,128)(2,1)} %param.19) | copy-start | bytes 9437188
  139.0 1.9 copy-start.5
  162.4 7.8 %copy-start.3 = (f32[32,2]{0,1:T(2,128)S(1)}, f32[32,2]{0,1:T(2,128)}, u32[]{:S(2)}) copy-start(f32[32,2]{0,1:T(2,128)} %param.17) | copy-start | bytes 772
  164.4 32.1 %all-to-all-start.1 = ((bf16[8,32,2048]{2,1,0:T(8,128)(2,1)}), bf16[8,32,2048]{2,1,0:T(8,128)(2,1)}, u32[]{:S(2)}, u32[]{:S(2)}) async-start(bf16[8,32,2048]{2,1,0:T(8,128)(2,1)} %fusion.10), calls=%async_computation.1 | async-start | bytes 2097152 | tf_op jit(solution)/shard_map/all_to_all | solution.py:104
Sparse Core Ops, SparseCore 0:
  9.5 42.8 all-gather.2
  54.5 38.8 all-gather.4
  142.7 18.2 all-reduce.3
where the time goes:
time: 209 us
  waiting for transfers between devices  95.2 us (46%)
  blocking collectives  54.9 us (26%)
  matrix products  22.6 us (11%)
  between operations  13.9 us (7%)
  local copies, waits for them, and re-layouts  12 us (6%)
  starting transfers between devices  5.86 us (3%)
  other arithmetic  4.33 us (2%)
    all_gather x1, waiting for transfers between devices, local(): lax.all_gather(values, 'ranks', axis=0, tiled=True)  33.4 us
    all_to_all x1, blocking collectives, local(): lax.all_to_all(outgoing.reshape(rank_total, capacity, half_width), 'ranks...  29.3 us
    all_to_all x1, waiting for transfers between devices, local(): lax.all_to_all(partial_out.reshape(rank_total, capacity, half_width).asty...  25.9 us
    unnamed x1, blocking collectives  23.1 us
    psum x1, waiting for transfers between devices, local(): lax.psum(up_part.astype(jnp.bfloat16), 'side').astype(jnp.float32)  18.5 us
    all_gather x1, waiting for transfers between devices, local(): lax.all_gather(keys, 'ranks', axis=0, tiled=True)  16.1 us
    all_to_all x1, starting transfers between devices, local(): lax.all_to_all(partial_out.reshape(rank_total, capacity, half_width).asty...  5.78 us
    dot_general x1, matrix products, local(): jnp.einsum('hqk,khd->hqd', weights.astype(jnp.bfloat16), all_values.resha...  5.01 us
  transfers between devices with their start and end apart: 4, of which 4 were waited for; matrix products, arithmetic and copies ran while one was open for 5% of the time, Pallas kernels for 0%

commit v1 on v0

--- a/solution.py
+++ b/solution.py
@@ -1,13 +1,19 @@
+import functools
 import math
 
 import jax
 import jax.numpy as jnp
 from jax import lax
+from jax.experimental import pallas as pl
+from jax.experimental.pallas import tpu as pltpu
 from jax.sharding import PartitionSpec as P
 
 D = 4096
 HEAD_DIM = 128
 TOP = 2
+
+
+CHUNK = 512
 
 
 def local(
@@ -115,9 +121,463 @@
     return layer_out.astype(jnp.bfloat16)
 
 
+BF16 = jnp.bfloat16
+F32 = jnp.float32
+COLUMNS = 2
+
+
+def dot(a, b, contract=((1,), (0,))):
+    return lax.dot_general(a, b, (contract, ((), ())), preferred_element_type=F32)
+
+
+def split_dot(a, b, contract=((1,), (0,))):
+    high = b.astype(BF16)
+    low = (b - high.astype(F32)).astype(BF16)
+    return dot(a, high, contract) + dot(a, low, contract)
+
+
+def layer_kernel(
+    ranks,
+    chunks,
+    q_hbm,
+    res_hbm,
+    k_ref,
+    v_ref,
+    map_ref,
+    ids_ref,
+    gates_ref,
+    gain_ref,
+    wg_hbm,
+    wu_hbm,
+    wd_hbm,
+    out_hbm,
+    q_ref,
+    res_ref,
+    wg_ref,
+    wu_ref,
+    wd_ref,
+    out_ref,
+    kv,
+    rows_all,
+    misc,
+    squares,
+    square_pair,
+    summed,
+    gate_acc,
+    up_acc,
+    pair_out,
+    pair_in,
+    part,
+    x_out,
+    x_in,
+    z_out,
+    z_in,
+    local_sem,
+    out_sem,
+    kv_send,
+    kv_recv,
+    row_send,
+    row_recv,
+    misc_send,
+    misc_recv,
+    sq_send,
+    sq_recv,
+    pair_send,
+    pair_recv,
+    x_send,
+    x_recv,
+    z_send,
+    z_recv,
+):
+    me = lax.axis_index("ranks")
+    side = lax.axis_index("side")
+    line = ranks // COLUMNS
+    z, x = me // COLUMNS, lax.rem(me, COLUMNS)
+    merged = k_ref.shape[0]
+    tokens, half = q_hbm.shape
+    width = half // chunks
+    slots = ranks * merged
+    factor = 1.0 / math.sqrt(HEAD_DIM)
+
+    def rank_at(dz):
+        return lax.rem(z + dz + line, line) * COLUMNS + x
+
+    across = z * COLUMNS + (1 - x)
+
+    def remote(src, dst, send, recv, target):
+        return pltpu.make_async_remote_copy(
+            src_ref=src,
+            dst_ref=dst,
+            send_sem=send,
+            recv_sem=recv,
+            device_id=target,
+            device_id_type=pl.DeviceIdType.MESH,
+        )
+
+    loads = [
+        pltpu.make_async_copy(src, dst, local_sem.at[i])
+        for i, (src, dst) in enumerate(
+            [
+                (q_hbm, q_ref),
+                (res_hbm, res_ref),
+                (wg_hbm, wg_ref),
+                (wu_hbm, wu_ref),
+                (wd_hbm, wd_ref),
+            ]
+        )
+    ]
+
+    barrier = pltpu.get_barrier_semaphore()
+    for dz in range(1, line):
+        pl.semaphore_signal(
+            barrier, inc=1, device_id={"ranks": rank_at(dz)}, device_id_type=pl.DeviceIdType.MESH
+        )
+    pl.semaphore_signal(
+        barrier, inc=1, device_id={"ranks": across}, device_id_type=pl.DeviceIdType.MESH
+    )
+    pl.semaphore_signal(
+        barrier, inc=1, device_id={"side": 1 - side}, device_id_type=pl.DeviceIdType.MESH
+    )
+
+    for c in range(chunks):
+        cols = slice(c * width, (c + 1) * width)
+        kv[me, c, 0:merged, :] = k_ref[:, cols]
+        kv[me, c, merged : 2 * merged, :] = v_ref[:, cols]
+
+    def own_copies(view, send, recv):
+        copies = [
+            remote(view(me), view(me), send(dz - 1), recv(dz - 1), {"ranks": rank_at(dz)})
+            for dz in range(1, line)
+        ]
+        copies.append(
+            remote(view(me), view(me), send(line - 1), recv(line - 1), {"ranks": across})
+        )
+        return copies
+
+    def forward(view, send, recv, dz):
+        came = view(rank_at(-dz))
+        return remote(came, came, send(line - 1 + dz), recv(line - 1 + dz), {"ranks": across})
+
+    def arrival(view, recv, send, dz):
+        came = view(rank_at(-dz))
+        return remote(came, came, send(dz - 1), recv(dz - 1), {"ranks": rank_at(dz)})
+
+    def crossed(view, recv, send, dz):
+        came = view(lax.rem(z - dz + line, line) * COLUMNS + (1 - x))
+        return remote(came, came, send(line - 1 + dz), recv(line - 1 + dz), {"ranks": across})
+
+    def spread(view, send, recv):
+        for copy in own_copies(view, send, recv):
+            copy.start()
+
+    def pass_on(view, send, recv):
+        for dz in range(1, line):
+            arrival(view, recv, send, dz).wait_recv()
+            forward(view, send, recv, dz).start()
+
+    def complete(view, send, recv):
+        for dz in range(line):
+            crossed(view, recv, send, dz).wait_recv()
+
+    def finish(view, send, recv):
+        for copy in own_copies(view, send, recv):
+            copy.wait_send()
+        for dz in range(1, line):
+            forward(view, send, recv, dz).wait_send()
+
+    def net(ref, send, recv, c=None):
+        if c is None:
+            return (lambda r: ref.at[r]), (lambda i: send.at[i]), (lambda i: recv.at[i])
+        return (lambda r: ref.at[r, c]), (lambda i: send.at[c, i]), (lambda i: recv.at[c, i])
+
+    kv_net = [net(kv, kv_send, kv_recv, c) for c in range(chunks)]
+    row_net = [net(rows_all, row_send, row_recv, c) for c in range(chunks)]
+    misc_net = net(misc, misc_send, misc_recv)
+    sq_net = net(squares, sq_send, sq_recv)
+
+    token_group = map_ref[...]
+    members = (
+        lax.broadcasted_iota(jnp.int32, (merged, tokens), 0) == token_group
+    ).astype(F32)
+    counts = jnp.sum(members, axis=1, keepdims=True)
+    members = members.astype(BF16)
+    own_lane = lax.broadcasted_iota(
+        jnp.int32, (merged, slots), 0
+    ) + me * merged == lax.broadcasted_iota(jnp.int32, (merged, slots), 1)
+
+    def as_row(column):
+        return jnp.sum(jnp.where(own_lane, column, 0.0), axis=0, keepdims=True)
+
+    row_id = lax.broadcasted_iota(jnp.int32, (8, slots), 0)
+    table = jnp.where(row_id == 7, as_row(jnp.log(counts).astype(BF16).astype(F32)), 0.0)
+    ids, gates = ids_ref[...], gates_ref[...]
+    for e in range(ranks // 2):
+        share = jnp.sum(jnp.where(ids == e, gates, 0.0), axis=1, keepdims=True)
+        table = table + jnp.where(row_id == e, as_row(share), 0.0)
+    misc[me] = table
+
+    pl.semaphore_wait(barrier, line + 1)
+    spread(*kv_net[0])
+    spread(*misc_net)
+    for c in range(1, chunks):
+        spread(*kv_net[c])
+    for load in loads:
+        load.start()
+
+    pass_on(*misc_net)
+    pass_on(*kv_net[0])
+    complete(*misc_net)
+    everything = jnp.sum(misc[...], axis=0)
+    bias = everything[7:8, :]
+    diagonal = lax.broadcasted_iota(jnp.int32, (slots, slots), 0) == lax.broadcasted_iota(
+        jnp.int32, (slots, slots), 1
+    )
+
+    def as_column(row):
+        return jnp.sum(jnp.where(diagonal, row, 0.0), axis=1, keepdims=True)
+
+    my_share = as_column(
+        jnp.sum(jnp.where(row_id == me // 2, everything, 0.0), axis=0, keepdims=True)
+    )
+
+    loads[0].wait()
+    loads[1].wait()
+    square_sum = jnp.zeros((merged, 1), F32)
+
+    def project(c):
+        complete(*row_net[c])
+        inputs = rows_all[:, c].reshape(slots, width)
+        along = slice(c * width, (c + 1) * width)
+        gate = dot(inputs, wg_ref[along, :])
+        up = dot(inputs, wu_ref[along, :])
+        if c == 0:
+            gate_acc[...] = gate
+            up_acc[...] = up
+        else:
+            gate_acc[...] += gate
+            up_acc[...] += up
+
+    for c in range(chunks):
+        if c + 1 < chunks:
+            pass_on(*kv_net[c + 1])
+        complete(*kv_net[c])
+        for h in range(width // HEAD_DIM):
+            inner = slice(h * HEAD_DIM, (h + 1) * HEAD_DIM)
+            cols = slice(c * width + h * HEAD_DIM, c * width + (h + 1) * HEAD_DIM)
+            key = kv[:, c, 0:merged, inner].reshape(slots, HEAD_DIM)
+            value = kv[:, c, merged : 2 * merged, inner].reshape(slots, HEAD_DIM)
+            scores = dot(q_ref[:, cols], key, ((1,), (1,))) * factor + bias
+            probs = jnp.exp(scores - jnp.max(scores, axis=1, keepdims=True))
+            total = jnp.sum(probs, axis=1, keepdims=True)
+            attended = dot(probs.astype(BF16), value) / total
+            summed[:, cols] = res_ref[:, cols].astype(F32) + attended
+        cols = slice(c * width, (c + 1) * width)
+        state = split_dot(members, summed[:, cols]) / counts
+        square_sum = square_sum + jnp.sum(state * state, axis=1, keepdims=True)
+        rows_all[me, c] = (state * gain_ref[:, cols].astype(F32)).astype(BF16)
+        spread(*row_net[c])
+        if c == chunks - 1:
+            squares[me] = jnp.broadcast_to(as_row(square_sum), (8, slots))
+            spread(*sq_net)
+        if c == 1:
+            loads[2].wait()
+            loads[3].wait()
+        if c >= 1:
+            pass_on(*row_net[c - 1])
+        if c >= 2:
+            project(c - 2)
+
+    pass_on(*row_net[chunks - 1])
+    pass_on(*sq_net)
+    project(chunks - 2)
+    complete(*sq_net)
+    square_pair[0] = jnp.sum(squares[...], axis=0)
+    other = {"side": 1 - side}
+    pair_copies = [
+        remote(square_pair.at[0], square_pair.at[1], pair_send.at[2], pair_recv.at[2], other),
+        remote(pair_out.at[0], pair_in.at[0], pair_send.at[0], pair_recv.at[0], other),
+        remote(pair_out.at[1], pair_in.at[1], pair_send.at[1], pair_recv.at[1], other),
+    ]
+    pair_copies[0].start()
+    project(chunks - 1)
+    pair_out[0] = gate_acc[...].astype(BF16)
+    pair_copies[1].start()
+    pair_out[1] = up_acc[...].astype(BF16)
+    pair_copies[2].start()
+    pair_copies[0].wait_recv()
+    all_squares = square_pair[0] + square_pair[1]
+    inverse = as_column(lax.rsqrt(all_squares[0:1, :] / (2 * half) + 1e-06))
+    pair_copies[1].wait_recv()
+    gate = (gate_acc[...] + pair_in[0].astype(F32)) * inverse
+    gate = gate / (1.0 + jnp.exp(-gate))
+    pair_copies[2].wait_recv()
+    hidden = (gate * ((up_acc[...] + pair_in[1].astype(F32)) * inverse)).astype(BF16)
+    loads[4].wait()
+
+    x_copies = [
+        remote(x_out.at[c], x_in.at[c], x_send.at[c], x_recv.at[c], {"ranks": across})
+        for c in range(chunks)
+    ]
+    z_copies = [
+        [
+            remote(
+                z_out.at[c, dz - 1],
+                z_in.at[c, dz - 1],
+                z_send.at[c, dz - 1],
+                z_recv.at[c, dz - 1],
+                {"ranks": rank_at(dz)},
+            )
+            for dz in range(1, line)
+        ]
+        for c in range(chunks)
+    ]
+
+    def line_sums(c):
+        x_copies[c].wait_recv()
+        for dz in range(1, line):
+            z_out[c, dz - 1] = (part[c, rank_at(dz)] + x_in[c, dz].astype(F32)).astype(BF16)
+            z_copies[c][dz - 1].start()
+
+    for c in range(chunks):
+        cols = slice(c * width, (c + 1) * width)
+        result = dot(hidden, wd_ref[:, cols]) * my_share
+        part[c] = result.reshape(ranks, merged, width)
+        for dz in range(line):
+            there = lax.rem(z + dz, line) * COLUMNS + (1 - x)
+            x_out[c, dz] = part[c, there].astype(BF16)
+        x_copies[c].start()
+    for c in range(chunks):
+        line_sums(c)
+    stores = []
+    for c in range(chunks):
+        cols = slice(c * width, (c + 1) * width)
+        expert_out = part[c, me] + x_in[c, 0].astype(F32)
+        for dz in range(1, line):
+            z_copies[c][dz - 1].wait_recv()
+            expert_out = expert_out + z_in[c, dz - 1].astype(F32)
+        out_ref[:, cols] = (
+            summed[:, cols] + split_dot(members, expert_out, ((0,), (0,)))
+        ).astype(BF16)
+        store = pltpu.make_async_copy(
+            out_ref.at[:, pl.ds(c * width, width)],
+            out_hbm.at[:, pl.ds(c * width, width)],
+            out_sem.at[c],
+        )
+        store.start()
+        stores.append(store)
+
+    for c in range(chunks):
+        finish(*kv_net[c])
+        finish(*row_net[c])
+        x_copies[c].wait_send()
+        for copy in z_copies[c]:
+            copy.wait_send()
+    finish(*misc_net)
+    finish(*sq_net)
+    for copy in pair_copies:
+        copy.wait_send()
+    for store in stores:
+        store.wait()
+
+
+def fused(
+    queries,
+    keys,
+    values,
+    residual,
+    merge_map,
+    expert_ids,
+    gate_weights,
+    norm_gain,
+    w_gate,
+    w_up,
+    w_down,
+):
+    ranks = lax.axis_size("ranks")
+    tokens, half = queries.shape
+    merged = keys.shape[0]
+    hidden = w_gate.shape[2]
+    chunks = half // CHUNK
+    line = ranks // COLUMNS
+    slots = ranks * merged
+    vmem = pl.BlockSpec(memory_space=pltpu.VMEM)
+    anywhere = pl.BlockSpec(memory_space=pl.ANY)
+    dma = pltpu.SemaphoreType.DMA
+    hops = 2 * line - 1
+    return pl.pallas_call(
+        functools.partial(layer_kernel, ranks, chunks),
+        out_shape=jax.ShapeDtypeStruct((tokens, half), BF16),
+        in_specs=[anywhere] * 2 + [vmem] * 6 + [anywhere] * 3,
+        out_specs=anywhere,
+        scratch_shapes=[
+            pltpu.VMEM((tokens, half), BF16),
+            pltpu.VMEM((tokens, half), BF16),
+            pltpu.VMEM((half, hidden), BF16),
+            pltpu.VMEM((half, hidden), BF16),
+            pltpu.VMEM((hidden, half), BF16),
+            pltpu.VMEM((tokens, half), BF16),
+            pltpu.VMEM((ranks, chunks, 2 * merged, CHUNK), BF16),
+            pltpu.VMEM((ranks, chunks, merged, CHUNK), BF16),
+            pltpu.VMEM((ranks, 8, slots), F32),
+            pltpu.VMEM((ranks, 8, slots), F32),
+            pltpu.VMEM((2, 8, slots), F32),
+            pltpu.VMEM((tokens, half), F32),
+            pltpu.VMEM((slots, hidden), F32),
+            pltpu.VMEM((slots, hidden), F32),
+            pltpu.VMEM((2, slots, hidden), BF16),
+            pltpu.VMEM((2, slots, hidden), BF16),
+            pltpu.VMEM((chunks, ranks, merged, CHUNK), F32),
+            pltpu.VMEM((chunks, line, merged, CHUNK), BF16),
+            pltpu.VMEM((chunks, line, merged, CHUNK), BF16),
+            pltpu.VMEM((chunks, line - 1, merged, CHUNK), BF16),
+            pltpu.VMEM((chunks, line - 1, merged, CHUNK), BF16),
+            dma((5,)),
+            dma((chunks,)),
+            dma((chunks, hops)),
+            dma((chunks, hops)),
+            dma((chunks, hops)),
+            dma((chunks, hops)),
+            dma((hops,)),
+            dma((hops,)),
+            dma((hops,)),
+            dma((hops,)),
+            dma((3,)),
+            dma((3,)),
+            dma((chunks,)),
+            dma((chunks,)),
+            dma((chunks, line - 1)),
+            dma((chunks, line - 1)),
+        ],
+        compiler_params=pltpu.CompilerParams(
+            collective_id=0, has_side_effects=True, vmem_limit_bytes=48 * 1024 * 1024
+        ),
+    )(
+        queries,
+        residual,
+        keys,
+        values,
+        merge_map.reshape(1, tokens),
+        expert_ids,
+        gate_weights,
+        norm_gain.reshape(1, half),
+        w_gate[0],
+        w_up[0],
+        w_down[0],
+    )
+
+
+def layer(*arrays):
+    ranks = lax.axis_size("ranks")
+    merged, half = arrays[1].shape
+    dense = 4 * merged // (ranks // 2) >= merged and ranks >= 4
+    if dense and half % CHUNK == 0 and half // CHUNK >= 2:
+        return fused(*arrays)
+    return local(*arrays)
+
+
 def solution(mesh):
     return jax.shard_map(
-        local,
+        layer,
         mesh=mesh,
         in_specs=(
             P(("groups", "ranks"), "side"),

time: 209 us -> 80.8 us (0.39)
  waiting for transfers between devices: 95.2 us -> 0 us
  Pallas kernels: 0 us -> 72.3 us
  blocking collectives: 54.9 us -> 0 us
  matrix products: 22.6 us -> 0 us
  between operations: 13.9 us -> 0.02 us
  starting transfers between devices: 5.86 us -> 0 us
  other arithmetic: 4.33 us -> 0 us
  local copies, waits for them, and re-layouts: 12 us -> 8.12 us
    pallas_call x0 -> x1, Pallas kernels: none -> 72.3 us  [fused(): pl.pallas_call(functools.partial(layer_kernel, ranks, chunks), out_shape=...]
    all_gather x2 -> x0, waiting for transfers between devices: 49.5 us -> none  [the longest x1 33.4 us: local(): lax.all_gather(values, 'ranks', axis=0, tiled=True)]
    all_to_all x1 -> x0, blocking collectives: 29.3 us -> none  [local(): lax.all_to_all(outgoing.reshape(rank_total, capacity, half_width), 'ranks...]
    all_to_all x1 -> x0, waiting for transfers between devices: 25.9 us -> none  [local(): lax.all_to_all(partial_out.reshape(rank_total, capacity, half_width).asty...]
    unnamed x1 -> x0, blocking collectives: 23.1 us -> none
    dot_general x10 -> x0, matrix products: 22.6 us -> none  [the longest x1 5.01 us: local(): jnp.einsum('hqk,khd->hqd', weights.astype(jnp.bfloat16), all_values.resha...]
    psum x1 -> x0, waiting for transfers between devices: 18.5 us -> none  [local(): lax.psum(up_part.astype(jnp.bfloat16), 'side').astype(jnp.float32)]
    all_to_all x1 -> x0, starting transfers between devices: 5.78 us -> none  [local(): lax.all_to_all(partial_out.reshape(rank_total, capacity, half_width).asty...]
  transfers between devices with their start and end apart: 4 -> 0, of which waited for: 4 -> 0; matrix products, arithmetic and copies ran while one was open for 5% -> 0% of each run, Pallas kernels for 0% -> 0%
where the time goes in v1:
time: 80.8 us; the launch traced here: 80.5 us
  Pallas kernels  72.3 us (89%)
  local copies, waits for them, and re-layouts  8.12 us (10%)
    pallas_call x1, Pallas kernels, fused(): pl.pallas_call(functools.partial(layer_kernel, ranks, chunks), out_shape=...  72.3 us
    unnamed x13, local copies, waits for them, and re-layouts  7.42 us

profile of v1, /device:TPU:0, one launch (start us, length us, event | category | flops | bytes accessed | tf_op | source)
XLA Modules:
  0.0 80.5 jit_solution(15458741161698033617)
XLA Ops:
  0.0 0.7 reshape.7.gain_ref
  0.7 0.8 copy.12.ids_ref
  1.5 0.8 copy.13.gates_ref
  2.2 0.0 copy-start
  2.2 1.2 %copy-done = bf16[256,2048]{1,0:T(8,128)(2,1)S(1)} copy-done((bf16[256,2048]{1,0:T(8,128)(2,1)S(1)}, bf16[256,2048]{1,0:T(8,128)(2,1)}, u32[]{:S(2)}) %copy-start) | copy-done | bytes 1048600
  3.4 0.0 copy-start.1
  3.4 1.2 %copy-done.1 = bf16[256,2048]{1,0:T(8,128)(2,1)S(1)} copy-done((bf16[256,2048]{1,0:T(8,128)(2,1)S(1)}, bf16[256,2048]{1,0:T(8,128)(2,1)}, u32[]{:S(2)}) %copy-start.1) | copy-done | bytes 1048600
  4.7 0.0 copy-start.2
  4.7 0.9 %copy-done.2 = bf16[32,2048]{1,0:T(8,128)(2,1)S(1)} copy-done((bf16[32,2048]{1,0:T(8,128)(2,1)S(1)}, bf16[32,2048]{1,0:T(8,128)(2,1)}, u32[]{:S(2)}) %copy-start.2) | copy-done | bytes 131096
  5.6 0.0 copy-start.3
  5.6 0.9 %copy-done.3 = bf16[32,2048]{1,0:T(8,128)(2,1)S(1)} copy-done((bf16[32,2048]{1,0:T(8,128)(2,1)S(1)}, bf16[32,2048]{1,0:T(8,128)(2,1)}, u32[]{:S(2)}) %copy-start.3) | copy-done | bytes 131096
  6.5 0.0 copy-start.4
  6.5 0.7 copy-done.4
  7.2 72.3 %shard_map.109 = bf16[256,2048]{1,0:T(8,128)(2,1)S(1)} custom-call(bf16[256,2048]{1,0:T(8,128)(2,1)S(1)} %copy-done, bf16[256,2048]{1,0:T(8,128)(2,1)S(1)} %copy-done.1, bf16[32,2048]{1,0:T(8,128)(2,1)S(1)} %copy-done.2, bf16[32,2048]{1,0:T(8,128)(2,1)S(1)} %copy-done.3, s32[1,256]{1,0:T(1,128)S(1)} %bitcast.4, s32[32,2]{1,0:T(8,128)S(1)} %copy.12.ids_ref, ...), custom_call_target="tpu_custom_call" | custom-call | tf_op jit(solution)/shard_map/pallas_call | solution.py:507
  79.5 1.0 %copy.15 = bf16[256,2048]{1,0:T(8,128)(2,1)} copy(bf16[256,2048]{1,0:T(8,128)(2,1)S(1)} %shard_map.109) | data formatting | bytes 2097152
Async XLA Ops:
  2.2 1.2 %copy-start = (bf16[256,2048]{1,0:T(8,128)(2,1)S(1)}, bf16[256,2048]{1,0:T(8,128)(2,1)}, u32[]{:S(2)}) copy-start(bf16[256,2048]{1,0:T(8,128)(2,1)} %q_hbm.1) | copy-start | bytes 3145732
  3.4 1.2 %copy-start.1 = (bf16[256,2048]{1,0:T(8,128)(2,1)S(1)}, bf16[256,2048]{1,0:T(8,128)(2,1)}, u32[]{:S(2)}) copy-start(bf16[256,2048]{1,0:T(8,128)(2,1)} %res_hbm.1) | copy-start | bytes 3145732
  4.7 0.9 %copy-start.2 = (bf16[32,2048]{1,0:T(8,128)(2,1)S(1)}, bf16[32,2048]{1,0:T(8,128)(2,1)}, u32[]{:S(2)}) copy-start(bf16[32,2048]{1,0:T(8,128)(2,1)} %k_ref.1) | copy-start | bytes 393220
  5.6 0.9 %copy-start.3 = (bf16[32,2048]{1,0:T(8,128)(2,1)S(1)}, bf16[32,2048]{1,0:T(8,128)(2,1)}, u32[]{:S(2)}) copy-start(bf16[32,2048]{1,0:T(8,128)(2,1)} %v_ref.1) | copy-start | bytes 393220
  6.5 0.7 copy-start.4

commit v2 on v1

--- a/solution.py
+++ b/solution.py
@@ -14,6 +14,8 @@
 
 
 CHUNK = 512
+WINDOW = 1
+SUM_WINDOW = 2
 
 
 def local(
@@ -141,16 +143,22 @@
     chunks,
     q_hbm,
     res_hbm,
+    k_hbm,
+    v_hbm,
+    map_hbm,
+    ids_hbm,
+    gates_hbm,
+    gain_hbm,
+    wg_hbm,
+    wu_hbm,
+    wd_hbm,
+    out_hbm,
     k_ref,
     v_ref,
     map_ref,
     ids_ref,
     gates_ref,
     gain_ref,
-    wg_hbm,
-    wu_hbm,
-    wd_hbm,
-    out_hbm,
     q_ref,
     res_ref,
     wg_ref,
@@ -193,7 +201,7 @@
     side = lax.axis_index("side")
     line = ranks // COLUMNS
     z, x = me // COLUMNS, lax.rem(me, COLUMNS)
-    merged = k_ref.shape[0]
+    merged = k_hbm.shape[0]
     tokens, half = q_hbm.shape
     width = half // chunks
     slots = ranks * merged
@@ -223,9 +231,18 @@
                 (wg_hbm, wg_ref),
                 (wu_hbm, wu_ref),
                 (wd_hbm, wd_ref),
+                (k_hbm, k_ref),
+                (v_hbm, v_ref),
+                (map_hbm, map_ref),
+                (ids_hbm, ids_ref),
+                (gates_hbm, gates_ref),
+                (gain_hbm, gain_ref),
             ]
         )
     ]
+
+    for load in loads[5:]:
+        load.start()
 
     barrier = pltpu.get_barrier_semaphore()
     for dz in range(1, line):
@@ -239,6 +256,8 @@
         barrier, inc=1, device_id={"side": 1 - side}, device_id_type=pl.DeviceIdType.MESH
     )
 
+    loads[5].wait()
+    loads[6].wait()
     for c in range(chunks):
         cols = slice(c * width, (c + 1) * width)
         kv[me, c, 0:merged, :] = k_ref[:, cols]
@@ -275,6 +294,11 @@
             arrival(view, recv, send, dz).wait_recv()
             forward(view, send, recv, dz).start()
 
+    def advance(c):
+        pass_on(*kv_net[c])
+        if c + WINDOW < chunks:
+            spread(*kv_net[c + WINDOW])
+
     def complete(view, send, recv):
         for dz in range(line):
             crossed(view, recv, send, dz).wait_recv()
@@ -295,6 +319,13 @@
     misc_net = net(misc, misc_send, misc_recv)
     sq_net = net(squares, sq_send, sq_recv)
 
+    pl.semaphore_wait(barrier, line + 1)
+    for c in range(min(WINDOW, chunks)):
+        spread(*kv_net[c])
+    for load in loads[:5]:
+        load.start()
+    for load in loads[7:]:
+        load.wait()
     token_group = map_ref[...]
     members = (
         lax.broadcasted_iota(jnp.int32, (merged, tokens), 0) == token_group
@@ -309,23 +340,20 @@
         return jnp.sum(jnp.where(own_lane, column, 0.0), axis=0, keepdims=True)
 
     row_id = lax.broadcasted_iota(jnp.int32, (8, slots), 0)
+    square = lax.broadcasted_iota(jnp.int32, (merged, merged), 0) == lax.broadcasted_iota(
+        jnp.int32, (merged, merged), 1
+    )
     table = jnp.where(row_id == 7, as_row(jnp.log(counts).astype(BF16).astype(F32)), 0.0)
     ids, gates = ids_ref[...], gates_ref[...]
     for e in range(ranks // 2):
-        share = jnp.sum(jnp.where(ids == e, gates, 0.0), axis=1, keepdims=True)
+        share = jnp.sum(jnp.where(ids == e, gates, 0.0), axis=0, keepdims=True)
+        share = jnp.sum(jnp.where(square, share, 0.0), axis=1, keepdims=True)
         table = table + jnp.where(row_id == e, as_row(share), 0.0)
     misc[me] = table
 
-    pl.semaphore_wait(barrier, line + 1)
-    spread(*kv_net[0])
     spread(*misc_net)
-    for c in range(1, chunks):
-        spread(*kv_net[c])
-    for load in loads:
-        load.start()
-
     pass_on(*misc_net)
-    pass_on(*kv_net[0])
+    advance(0)
     complete(*misc_net)
     everything = jnp.sum(misc[...], axis=0)
     bias = everything[7:8, :]
@@ -343,6 +371,12 @@
     loads[0].wait()
     loads[1].wait()
     square_sum = jnp.zeros((merged, 1), F32)
+    heads = width // HEAD_DIM
+
+    def gain_row(c):
+        rows = [gain_ref[c * heads + h : c * heads + h + 1, :] for h in range(heads)]
+        return jnp.concatenate(rows, axis=1).astype(F32)
+
 
     def project(c):
         complete(*row_net[c])
@@ -359,9 +393,9 @@
 
     for c in range(chunks):
         if c + 1 < chunks:
-            pass_on(*kv_net[c + 1])
+            advance(c + 1)
         complete(*kv_net[c])
-        for h in range(width // HEAD_DIM):
+        for h in range(heads):
             inner = slice(h * HEAD_DIM, (h + 1) * HEAD_DIM)
             cols = slice(c * width + h * HEAD_DIM, c * width + (h + 1) * HEAD_DIM)
             key = kv[:, c, 0:merged, inner].reshape(slots, HEAD_DIM)
@@ -374,7 +408,7 @@
         cols = slice(c * width, (c + 1) * width)
         state = split_dot(members, summed[:, cols]) / counts
         square_sum = square_sum + jnp.sum(state * state, axis=1, keepdims=True)
-        rows_all[me, c] = (state * gain_ref[:, cols].astype(F32)).astype(BF16)
+        rows_all[me, c] = (state * gain_row(c)).astype(BF16)
         spread(*row_net[c])
         if c == chunks - 1:
             squares[me] = jnp.broadcast_to(as_row(square_sum), (8, slots))
@@ -414,8 +448,18 @@
     hidden = (gate * ((up_acc[...] + pair_in[1].astype(F32)) * inverse)).astype(BF16)
     loads[4].wait()
 
+    far, near = pl.ds(1, line - 1), pl.ds(0, 1)
     x_copies = [
-        remote(x_out.at[c], x_in.at[c], x_send.at[c], x_recv.at[c], {"ranks": across})
+        [
+            remote(
+                x_out.at[c, blocks],
+                x_in.at[c, blocks],
+                x_send.at[c, i],
+                x_recv.at[c, i],
+                {"ranks": across},
+            )
+            for i, blocks in enumerate((far, near))
+        ]
         for c in range(chunks)
     ]
     z_copies = [
@@ -432,25 +476,31 @@
         for c in range(chunks)
     ]
 
-    def line_sums(c):
-        x_copies[c].wait_recv()
-        for dz in range(1, line):
-            z_out[c, dz - 1] = (part[c, rank_at(dz)] + x_in[c, dz].astype(F32)).astype(BF16)
-            z_copies[c][dz - 1].start()
-
-    for c in range(chunks):
+    def column_part(c):
         cols = slice(c * width, (c + 1) * width)
         result = dot(hidden, wd_ref[:, cols]) * my_share
         part[c] = result.reshape(ranks, merged, width)
         for dz in range(line):
             there = lax.rem(z + dz, line) * COLUMNS + (1 - x)
             x_out[c, dz] = part[c, there].astype(BF16)
-        x_copies[c].start()
+        x_copies[c][0].start()
+
+    for c in range(min(SUM_WINDOW, chunks)):
+        column_part(c)
     for c in range(chunks):
-        line_sums(c)
+        x_copies[c][0].wait_recv()
+        if c + SUM_WINDOW < chunks:
+            column_part(c + SUM_WINDOW)
+        if c == max(0, chunks - 1 - SUM_WINDOW):
+            for last in range(chunks):
+                x_copies[last][1].start()
+        for dz in range(1, line):
+            z_out[c, dz - 1] = (part[c, rank_at(dz)] + x_in[c, dz].astype(F32)).astype(BF16)
+            z_copies[c][dz - 1].start()
     stores = []
     for c in range(chunks):
         cols = slice(c * width, (c + 1) * width)
+        x_copies[c][1].wait_recv()
         expert_out = part[c, me] + x_in[c, 0].astype(F32)
         for dz in range(1, line):
             z_copies[c][dz - 1].wait_recv()
@@ -469,7 +519,8 @@
     for c in range(chunks):
         finish(*kv_net[c])
         finish(*row_net[c])
-        x_copies[c].wait_send()
+        for copy in x_copies[c]:
+            copy.wait_send()
         for copy in z_copies[c]:
             copy.wait_send()
     finish(*misc_net)
@@ -500,16 +551,21 @@
     chunks = half // CHUNK
     line = ranks // COLUMNS
     slots = ranks * merged
-    vmem = pl.BlockSpec(memory_space=pltpu.VMEM)
     anywhere = pl.BlockSpec(memory_space=pl.ANY)
     dma = pltpu.SemaphoreType.DMA
     hops = 2 * line - 1
     return pl.pallas_call(
         functools.partial(layer_kernel, ranks, chunks),
         out_shape=jax.ShapeDtypeStruct((tokens, half), BF16),
-        in_specs=[anywhere] * 2 + [vmem] * 6 + [anywhere] * 3,
+        in_specs=[anywhere] * 11,
         out_specs=anywhere,
         scratch_shapes=[
+            pltpu.VMEM((merged, half), BF16),
+            pltpu.VMEM((merged, half), BF16),
+            pltpu.VMEM((1, tokens), jnp.int32),
+            pltpu.VMEM((TOP, merged), jnp.int32),
+            pltpu.VMEM((TOP, merged), F32),
+            pltpu.VMEM((half // HEAD_DIM, HEAD_DIM), BF16),
             pltpu.VMEM((tokens, half), BF16),
             pltpu.VMEM((tokens, half), BF16),
             pltpu.VMEM((half, hidden), BF16),
@@ -531,7 +587,7 @@
             pltpu.VMEM((chunks, line, merged, CHUNK), BF16),
             pltpu.VMEM((chunks, line - 1, merged, CHUNK), BF16),
             pltpu.VMEM((chunks, line - 1, merged, CHUNK), BF16),
-            dma((5,)),
+            dma((11,)),
             dma((chunks,)),
             dma((chunks, hops)),
             dma((chunks, hops)),
@@ -543,13 +599,13 @@
             dma((hops,)),
             dma((3,)),
             dma((3,)),
-            dma((chunks,)),
-            dma((chunks,)),
+            dma((chunks, 2)),
+            dma((chunks, 2)),
             dma((chunks, line - 1)),
             dma((chunks, line - 1)),
         ],
         compiler_params=pltpu.CompilerParams(
-            collective_id=0, has_side_effects=True, vmem_limit_bytes=48 * 1024 * 1024
+            collective_id=0, has_side_effects=True, vmem_limit_bytes=60 * 1024 * 1024
         ),
     )(
         queries,
@@ -557,9 +613,9 @@
         keys,
         values,
         merge_map.reshape(1, tokens),
-        expert_ids,
-        gate_weights,
-        norm_gain.reshape(1, half),
+        expert_ids.T,
+        gate_weights.T,
+        norm_gain.reshape(half // HEAD_DIM, HEAD_DIM),
         w_gate[0],
         w_up[0],
         w_down[0],

time: 80.8 us -> 73.8 us (0.913)
  local copies, waits for them, and re-layouts: 8.12 us -> 2.3 us
  Pallas kernels: 72.3 us -> 71.1 us
    unnamed x13 -> x1, local copies, waits for them, and re-layouts: 7.42 us -> 2.3 us
    pallas_call x1, Pallas kernels: 72.3 us -> 71.1 us  [fused(): pl.pallas_call(functools.partial(layer_kernel, ranks, chunks), out_shape=...]
where the time goes in v2:
time: 73.8 us; the launch traced here: 73.4 us
  Pallas kernels  71.1 us (96%)
  local copies, waits for them, and re-layouts  2.3 us (3%)
    pallas_call x1, Pallas kernels, fused(): pl.pallas_call(functools.partial(layer_kernel, ranks, chunks), out_shape=...  71.1 us
    unnamed x1, local copies, waits for them, and re-layouts  2.3 us

profile of v2, /device:TPU:0, one launch (start us, length us, event | category | flops | bytes accessed | tf_op | source)
XLA Modules:
  0.0 73.4 jit_solution(7546580744345331051)
XLA Ops:
  0.0 71.1 %shard_map.109 = bf16[256,2048]{1,0:T(8,128)(2,1)} custom-call(bf16[256,2048]{1,0:T(8,128)(2,1)} %q_hbm.1, bf16[256,2048]{1,0:T(8,128)(2,1)} %res_hbm.1, bf16[32,2048]{1,0:T(8,128)(2,1)} %k_hbm.1, bf16[32,2048]{1,0:T(8,128)(2,1)} %v_hbm.1, s32[1,256]{1,0:T(1,128)} %bitcast.11, s32[2,32]{1,0:T(2,128)} %bitcast.12, f32[2,32]{1,0:T(2,128)} %bitcast.13, ...), custom_call_target="tpu_custom_call" | custom-call | tf_op jit(solution)/shard_map/pallas_call | solution.py:557
  71.1 2.3 %copy.13 = bf16[256,2048]{1,0:T(8,128)(2,1)} copy(bf16[256,2048]{1,0:T(8,128)(2,1)} %shard_map.109) | data formatting | bytes 2097152
